TPU v7x, 128 devices: a whole 4x4x4 slice. The times are simulated.
128 devices in a mesh: head: 4 (over x_lo, core), expert: 32 (over z, y, x_hi).
Axes of the slice: x: 4 (x_hi: 2, x_lo: 2; x = x_hi * 2 + x_lo), y: 4, z: 4, core: 2. Of those that a mesh axis runs over, the one named last changes fastest.
Arguments:
- attn: bfloat16 [4096, 4096], P('expert', 'head'), may hold values from -6 to 6
- o_weight: bfloat16 [4096, 4096], P('head'), may hold values from -0.09375 to 0.09375
- residual: bfloat16 [4096, 4096], P('expert'), may hold values from -6 to 6
- expert_ids: int32 [4096, 8], P('expert'), may hold values from 0 to 31, all different within a row; in each aligned block of 128 rows (0 to 127, 128 to 255, ...) at most 64 rows name the same one
- route_weight: bfloat16 [4096, 8], P('expert'), may hold values from 0.099609375 to 1
- gate_weight: bfloat16 [32, 4096, 1536], P('expert', None, 'head'), may hold values from -0.09375 to 0.09375
- up_weight: bfloat16 [32, 4096, 1536], P('expert', None, 'head'), may hold values from -0.09375 to 0.09375
Outputs:
- gram: float32 [32, 1536, 1536], P('expert', 'head')
Inputs may be any that keep to these rules, and one draw needn't show every extreme that they name: `expert_ids`: among the 128 rows of one device no expert is named more than 64 times, a bound that some block reaches; each row names 8 different experts.
All inputs are finite; a program needn't handle non-finite values.
Results may differ from a plain program's by a relative error of at most 0.0065.
Values may be sent and summed in bfloat16 or wider, within the bound.
No kernel may reach another device: no remote copies, remote signals or barrier semaphores. Data moves between devices by JAX's collectives and lax.ppermute only.
A program may use at most 128 MiB of HBM per device.

v0:
```python
import jax
import jax.numpy as jnp
from jax import lax
from jax.sharding import PartitionSpec as P


def body(attn, o_weight, residual, expert_ids, route_weight, gate_weight, up_weight):
    partial_value = jnp.dot(attn, o_weight, preferred_element_type=jnp.float32)
    width = residual.shape[1]
    mixed = residual.astype(jnp.float32) + lax.psum(partial_value, "head")
    squares = jnp.sum(mixed * mixed, axis=1)
    normed = (mixed * lax.rsqrt(squares / width + 1e-06)[:, None]).astype(jnp.bfloat16)
    owners = lax.axis_size("expert")
    tok_rows = expert_ids.shape[0]
    picks = expert_ids.shape[1]
    capacity = min(tok_rows, 2 * tok_rows * picks // owners)
    flat_ids = expert_ids.reshape(-1)
    hits = (flat_ids[:, None] == jnp.arange(owners, dtype=jnp.int32)[None, :]).astype(jnp.int32)
    before = jnp.cumsum(hits, axis=0) - hits
    rank = jnp.sum(before * hits, axis=1)
    slot_of = flat_ids * capacity + rank
    select = jnp.arange(owners * capacity, dtype=jnp.int32)[:, None] == slot_of[None, :]
    pick_rows = jnp.sum(
        select.reshape(owners * capacity, tok_rows, picks).astype(jnp.float32), axis=2
    ).astype(jnp.bfloat16)
    outgoing = jnp.dot(pick_rows, normed, preferred_element_type=jnp.float32).astype(jnp.bfloat16)
    out_weight = jnp.dot(
        select.astype(jnp.bfloat16), route_weight.reshape(-1), preferred_element_type=jnp.float32
    ).astype(jnp.bfloat16)
    outgoing = outgoing.reshape(owners, capacity, outgoing.shape[1])
    out_weight = out_weight.reshape(owners, capacity)
    received, got_weight = (
        lax.all_to_all(outgoing, "expert", split_axis=0, concat_axis=0, tiled=True),
        lax.all_to_all(out_weight, "expert", split_axis=0, concat_axis=0, tiled=True),
    )
    received = received.reshape(owners * capacity, received.shape[2])
    weights = got_weight.reshape(-1).astype(jnp.float32)
    w_gate = gate_weight[0]
    w_up = up_weight[0]
    gate = jnp.dot(received, w_gate, preferred_element_type=jnp.float32)
    up = jnp.dot(received, w_up, preferred_element_type=jnp.float32)
    keys = (jax.nn.silu(gate) * up).astype(jnp.bfloat16)
    scaled = (keys.astype(jnp.float32) * weights[:, None]).astype(jnp.bfloat16)
    total = jnp.sum(weights)
    block = lax.dot_general(
        scaled,
        lax.all_gather(keys, "head", axis=1, tiled=True),
        (((0,), (0,)), ((), ())),
        preferred_element_type=jnp.float32,
    )
    return (block / total)[None]


def solution(mesh):
    return jax.shard_map(
        body,
        mesh=mesh,
        in_specs=(
            P("expert", "head"),
            P("head", None),
            P("expert", None),
            P("expert", None),
            P("expert", None),
            P("expert", None, "head"),
            P("expert", None, "head"),
        ),
        out_specs=P("expert", "head", None),
        check_vma=False,
    )
```

profile of v0, /device:TPU:1, one launch (start us, length us, event | category | flops | bytes accessed | tf_op | source)
XLA Modules:
  0.0 379.8 jit_solution(18009387903659166094)
XLA Ops:
  6.5 0.0 copy-start
  6.5 0.0 copy-start.2
  6.5 0.0 all-reduce.2.cloned.1.call-start
  6.5 6.2 %fusion.16 = f32[128,4096]{1,0:T(8,128)} fusion(bf16[128,1024]{1,0:T(8,128)(2,1)} %param.7, bf16[1024,4096]{1,0:T(8,128)(2,1)} %param.8), kind=kOutput, calls=%fused_computation.33 | convolution fusion | flops 1073741824 | bytes 10747904 | tf_op jit(solution)/shard_map/dot_general | solution.py:8
  12.7 0.0 all-reduce.2.cloned.1.call-update
  12.8 0.0 all-gather.2.cloned.1.call-start
  12.8 0.0 copy-done.2
  12.8 0.1 copy.33
  12.9 0.1 eq.50
  13.0 0.1 eq.46
  13.1 9.0 %reduce-window.6 = s32[32,8,128]{2,1,0:T(8,128)S(1)} reduce-window(s32[32,8,128]{2,1,0:T(8,128)S(1)} %fusion.15, s32[]{:T(128)} %constant.7.clone.1), window={size=1x1x128 pad=0_0x0_0x127_0}, to_apply=%region_0.0 | reduce-window | flops 4161536 | bytes 262148 | tf_op jit(solution)/shard_map/reduce-window
  22.2 0.1 slice.8
  22.3 0.1 copy.35
  22.4 0.1 copy.36
  22.5 0.1 broadcast_add_fusion
  22.7 0.1 reduce_sum.39
  22.8 11.5 %convert_reduce_fusion = bf16[2048,128]{1,0:T(8,128)(2,1)} fusion(s32[128,8]{0,1:T(8,128)S(1)} %multiply_add_fusion.1), kind=kLoop, calls=%fused_computation.2 | loop fusion | flops 6029312 | bytes 528384 | tf_op jit(solution)/shard_map/reduce_sum | solution.py:23
  34.3 39.5 %all-reduce.2.cloned.1.call-done = f32[128,4096]{1,0:T(8,128)} async-done(((f32[128,4096]{1,0:T(8,128)}), f32[128,4096]{1,0:T(8,128)}) %all-reduce.2.cloned.1.call-update) | async-done | bytes 2097168 | tf_op jit(solution)/shard_map/psum | solution.py:10
  73.8 2.2 multiply_reduce_fusion
  76.0 12.3 %convolution_convert_fusion = bf16[2048,4096]{1,0:T(8,128)(2,1)} fusion(f32[128,4096]{1,0:T(8,128)} %all-reduce.2.cloned.1.call-done, bf16[128,4096]{1,0:T(8,128)(2,1)} %param.9, f32[128]{0:T(128)S(1)} %add_rsqrt_fusion, bf16[2048,128]{1,0:T(8,128)(2,1)} %convert_reduce_fusion), kind=kOutput, calls=%fused_computation | convolution fusion | flops 2157969408 | bytes 20447744 | tf_op jit(solution)/shard_map/dot_general | solution.py:26
  88.4 196.1 %all_to_all.15 = bf16[32,64,4096]{2,1,0:T(8,128)(2,1)S(1)} all-to-all(bf16[32,64,4096]{2,1,0:T(8,128)(2,1)} %bitcast.38), channel_id=1, replica_groups=mesh['head'=4,'expert'=32] {'expert'}, dimensions={0} | all-to-all | bytes 33554432 | tf_op jit(solution)/shard_map/all_to_all | solution.py:33
  284.5 0.0 copy-done
  284.5 0.0 copy-start.4
  284.5 8.9 %fusion.3 = f32[2048,384]{1,0:T(8,128)S(1)} fusion(bf16[2048,4096]{1,0:T(8,128)(2,1)S(1)} %bitcast.39, bf16[1,4096,384]{2,1,0:T(8,128)(2,1)S(1)} %copy-done), kind=kOutput, calls=%fused_computation.8 | convolution fusion | flops 6442450944 | bytes 23068672 | tf_op jit(solution)/shard_map/dot_general | solution.py:40
  293.4 0.0 copy-done.4
  293.4 0.0 copy-start.3
  293.4 10.0 %fusion.6 = bf16[2048,384]{1,0:T(8,128)(2,1)} fusion(bf16[2048,4096]{1,0:T(8,128)(2,1)S(1)} %bitcast.40, bf16[1,4096,384]{2,1,0:T(8,128)(2,1)S(1)} %copy-done.4, f32[2048,384]{1,0:T(8,128)S(1)} %fusion.3), kind=kOutput, calls=%fused_computation.13 | convolution fusion | flops 6447169536 | bytes 24641536 | tf_op jit(solution)/shard_map/dot_general | solution.py:41
  303.4 0.0 all-gather.2.cloned.1.call-update
  303.5 0.0 copy-done.3
  303.5 0.1 copy.38
  303.6 0.1 reshape.69
  303.7 1.5 fusion
  305.2 0.1 all_to_all.12
  305.3 12.0 %all_to_all.16 = bf16[32,1,64]{2,1,0:T(2,128)(2,1)S(1)} all-to-all(bf16[32,1,64]{2,1,0:T(2,128)(2,1)S(1)} %all_to_all.12), channel_id=1, replica_groups=mesh['head'=4,'expert'=32] {'expert'}, dimensions={0} | all-to-all | bytes 8192 | tf_op jit(solution)/shard_map/all_to_all | solution.py:34
  317.3 0.7 convert_reduce_fusion.1
  318.0 0.1 reshape.68
  318.1 46.6 %all-gather.2.cloned.1.call-done = bf16[2048,1536]{1,0:T(8,128)(2,1)} async-done(((bf16[2048,384]{1,0:T(8,128)(2,1)}), bf16[2048,1536]{1,0:T(8,128)(2,1)}) %all-gather.2.cloned.1.call-update) | async-done | bytes 6291472 | tf_op jit(solution)/shard_map/all_gather | solution.py:47
  364.7 0.0 copy-start.1
  364.7 8.3 %fusion.5 = f32[1,384,1536]{2,1,0:T(8,128)} fusion(bf16[2048,1536]{1,0:T(8,128)(2,1)} %all-gather.2.cloned.1.call-done, bf16[2048,384]{1,0:T(8,128)(2,1)} %fusion.6, f32[2048]{0:T(1024)S(1)} %reshape.68, f32[]{:T(128)} %get-tuple-element.5), kind=kOutput, calls=%fused_computation.12 | convolution fusion | flops 2418868224 | bytes 10231812 | tf_op jit(solution)/shard_map/dot_general | solution.py:45
  373.0 0.0 copy-done.1
  (9 shorter events, 0.2 us)
Async XLA Ops:
  6.5 278.0 %copy-start = (bf16[1,4096,384]{2,1,0:T(8,128)(2,1)S(1)}, bf16[1,4096,384]{2,1,0:T(8,128)(2,1)}, u32[]{:S(2)}) copy-start(bf16[1,4096,384]{2,1,0:T(8,128)(2,1)} %param.12) | copy-start | bytes 9437188
  6.5 6.3 %copy-start.2 = (s32[128,8]{0,1:T(8,128)S(1)}, s32[128,8]{0,1:T(8,128)}, u32[]{:S(2)}) copy-start(s32[128,8]{0,1:T(8,128)} %param.10) | copy-start | bytes 12292
  6.5 67.3 %all-reduce.2.cloned.1.call-start = ((), (), s32[]{:S(2)}) async-start(), calls=%async_computation.2 | async-start | bytes 4194304 | tf_op jit(solution)/shard_map/psum | solution.py:10
  12.8 351.9 %all-gather.2.cloned.1.call-start = ((), (), s32[]{:S(2)}) async-start(), calls=%async_computation.3 | async-start | bytes 7864320 | tf_op jit(solution)/shard_map/all_gather | solution.py:47
  284.5 8.9 %copy-start.4 = (bf16[1,4096,384]{2,1,0:T(8,128)(2,1)S(1)}, bf16[1,4096,384]{2,1,0:T(8,128)(2,1)}, u32[]{:S(2)}) copy-start(bf16[1,4096,384]{2,1,0:T(8,128)(2,1)} %param.13) | copy-start | bytes 9437188
  293.4 10.1 %copy-start.3 = (bf16[128,8]{0,1:T(8,128)(2,1)S(1)}, bf16[128,8]{0,1:T(8,128)(2,1)}, u32[]{:S(2)}) copy-start(bf16[128,8]{0,1:T(8,128)(2,1)} %param.11) | copy-start | bytes 6148
  364.7 8.3 %copy-start.1 = (bf16[1,4096,384]{2,1,0:T(8,128)(2,1)S(1)}, bf16[1,4096,384]{2,1,0:T(8,128)(2,1)}, u32[]{:S(2)}) copy-start(bf16[1,4096,384]{2,1,0:T(8,128)(2,1)} %param.12) | copy-start | bytes 9437188
Sparse Core Ops, SparseCore 0:
  12.9 60.8 all-reduce.1
  303.6 61.0 all-gather.1
where the time goes:
time: 380 us
  blocking collectives  208 us (55%)
  waiting for transfers between devices  86.1 us (23%)
  matrix products  47.2 us (12%)
  other arithmetic  23.7 us (6%)
  between operations  13.5 us (4%)
    all_to_all x1, blocking collectives, body(): lax.all_to_all(outgoing, 'expert', split_axis=0, concat_axis=0, tiled=True)  196 us
    all_gather x1, waiting for transfers between devices, body(): lax.all_gather(keys, 'head', axis=1, tiled=True)  46.6 us
    psum x1, waiting for transfers between devices, body(): mixed = residual.astype(jnp.float32) + lax.psum(partial_value, 'head')  39.5 us
    dot_general x1, matrix products, body(): jnp.dot(pick_rows, normed, preferred_element_type=jnp.float32)  12.3 us
    all_to_all x1, blocking collectives, body(): lax.all_to_all(out_weight, 'expert', split_axis=0, concat_axis=0, tiled=T...  12 us
    reduce_sum x1, other arithmetic, body(): jnp.sum(select.reshape(owners * capacity, tok_rows, picks).astype(jnp.flo...  11.5 us
    dot_general x1, matrix products, body(): up = jnp.dot(received, w_up, preferred_element_type=jnp.float32)  10 us
    another operation x3, other arithmetic  9.15 us
  transfers between devices with their start and end apart: 2, of which 2 were waited for; matrix products, arithmetic and copies ran while one was open for 6% of the time, Pallas kernels for 0%

commit v1 on v0

--- a/solution.py
+++ b/solution.py
@@ -44,7 +44,9 @@
     total = jnp.sum(weights)
     block = lax.dot_general(
         scaled,
-        lax.all_gather(keys, "head", axis=1, tiled=True),
+        jnp.concatenate(
+            lax.all_to_all(jnp.stack([keys] * lax.axis_size("head")), "head", 0, 0), axis=1
+        ),
         (((0,), (0,)), ((), ())),
         preferred_element_type=jnp.float32,
     )

time: 380 us -> 514 us (1.35)
  waiting for transfers between devices: 86.1 us -> 353 us
  blocking collectives: 208 us -> 0 us
  starting transfers between devices: 0.04 us -> 64.8 us
  matrix products: 47.2 us -> 53.2 us
    all_to_all x0 -> x3, waiting for transfers between devices: none -> 313 us  [the longest x1 244 us: body(): lax.all_to_all(outgoing, 'expert', split_axis=0, concat_axis=0, tiled=True)]
    all_to_all x2 -> x0, blocking collectives: 208 us -> none  [the longest x1 196 us: body(): lax.all_to_all(outgoing, 'expert', split_axis=0, concat_axis=0, tiled=True)]
    all_to_all x0 -> x3, starting transfers between devices: none -> 64.8 us  [the longest x1 48.2 us: body(): lax.all_to_all(out_weight, 'expert', split_axis=0, concat_axis=0, tiled=T...]
    all_gather x1 -> x0, waiting for transfers between devices: 46.6 us -> none  [body(): lax.all_gather(keys, 'head', axis=1, tiled=True)]
  transfers between devices with their start and end apart: 2 -> 4, of which waited for: 2 -> 3; matrix products, arithmetic and copies ran while one was open for 6% -> 10% of each run, Pallas kernels for 0% -> 0%
where the time goes in v1:
time: 514 us
  waiting for transfers between devices  353 us (69%)
  starting transfers between devices  64.8 us (13%)
  matrix products  53.2 us (10%)
  other arithmetic  23.6 us (5%)
  between operations  13.6 us (3%)
  local copies, waits for them, and re-layouts  5.95 us (1%)
    all_to_all x1, waiting for transfers between devices, body(): lax.all_to_all(outgoing, 'expert', split_axis=0, concat_axis=0, tiled=True)  244 us
    all_to_all x1, waiting for transfers between devices, body(): lax.all_to_all(jnp.stack([keys] * lax.axis_size('head')), 'head', 0, 0)  69.1 us
    all_to_all x1, starting transfers between devices, body(): lax.all_to_all(out_weight, 'expert', split_axis=0, concat_axis=0, tiled=T...  48.2 us
    psum x1, waiting for transfers between devices, body(): mixed = residual.astype(jnp.float32) + lax.psum(partial_value, 'head')  39.6 us
    dot_general x1, matrix products, body(): up = jnp.dot(received, w_up, preferred_element_type=jnp.float32)  12.6 us
    dot_general x1, matrix products, body(): jnp.dot(pick_rows, normed, preferred_element_type=jnp.float32)  12.3 us
    dot_general x1, matrix products, body(): gate = jnp.dot(received, w_gate, preferred_element_type=jnp.float32)  12.1 us
    reduce_sum x1, other arithmetic, body(): jnp.sum(select.reshape(owners * capacity, tok_rows, picks).astype(jnp.flo...  11.5 us
  transfers between devices with their start and end apart: 4, of which 3 were waited for; matrix products, arithmetic and copies ran while one was open for 10% of the time, Pallas kernels for 0%

profile of v1, /device:TPU:1, one launch (start us, length us, event | category | flops | bytes accessed | tf_op | source)
XLA Modules:
  0.0 513.9 jit_solution(13564832426878853049)
XLA Ops:
  6.5 0.0 copy-start
  6.5 0.0 copy-start.3
  6.5 0.0 all-reduce.2.cloned.1.call-start
  6.5 6.2 %fusion.16 = f32[128,4096]{1,0:T(8,128)} fusion(bf16[128,1024]{1,0:T(8,128)(2,1)} %param.7, bf16[1024,4096]{1,0:T(8,128)(2,1)} %param.8), kind=kOutput, calls=%fused_computation.33 | convolution fusion | flops 1073741824 | bytes 10747904 | tf_op jit(solution)/shard_map/dot_general | solution.py:8
  12.7 0.0 all-reduce.2.cloned.1.call-update
  12.8 0.0 copy-done.3
  12.8 0.1 copy.36
  12.9 0.1 eq.50
  13.0 0.1 eq.46
  13.1 9.0 %reduce-window.6 = s32[32,8,128]{2,1,0:T(8,128)S(1)} reduce-window(s32[32,8,128]{2,1,0:T(8,128)S(1)} %fusion.15, s32[]{:T(128)} %constant.7.clone.1), window={size=1x1x128 pad=0_0x0_0x127_0}, to_apply=%region_0.0 | reduce-window | flops 4161536 | bytes 262148 | tf_op jit(solution)/shard_map/reduce-window
  22.1 0.1 slice.8
  22.2 0.1 copy.38
  22.4 0.1 copy.39
  22.4 0.1 broadcast_add_fusion
  22.6 0.1 reduce_sum.39
  22.7 11.5 %convert_reduce_fusion = bf16[2048,128]{1,0:T(8,128)(2,1)} fusion(s32[128,8]{0,1:T(8,128)S(1)} %multiply_add_fusion.1), kind=kLoop, calls=%fused_computation.2 | loop fusion | flops 6029312 | bytes 528384 | tf_op jit(solution)/shard_map/reduce_sum | solution.py:23
  34.3 39.6 %all-reduce.2.cloned.1.call-done = f32[128,4096]{1,0:T(8,128)} async-done(((f32[128,4096]{1,0:T(8,128)}), f32[128,4096]{1,0:T(8,128)}) %all-reduce.2.cloned.1.call-update) | async-done | bytes 2097168 | tf_op jit(solution)/shard_map/psum | solution.py:10
  73.9 2.2 multiply_reduce_fusion
  76.1 12.3 %convolution_convert_fusion = bf16[2048,4096]{1,0:T(8,128)(2,1)} fusion(f32[128,4096]{1,0:T(8,128)} %all-reduce.2.cloned.1.call-done, bf16[128,4096]{1,0:T(8,128)(2,1)} %param.9, f32[128]{0:T(128)S(1)} %add_rsqrt_fusion, bf16[2048,128]{1,0:T(8,128)(2,1)} %convert_reduce_fusion), kind=kOutput, calls=%fused_computation | convolution fusion | flops 2157969408 | bytes 20447744 | tf_op jit(solution)/shard_map/dot_general | solution.py:26
  88.4 0.0 copy-start.4
  88.4 9.5 %all-to-all-start = ((bf16[32,64,4096]{2,1,0:T(8,128)(2,1)}), bf16[32,64,4096]{2,1,0:T(8,128)(2,1)}, u32[]{:S(2)}, u32[]{:S(2)}) async-start(bf16[32,64,4096]{2,1,0:T(8,128)(2,1)} %bitcast.41), calls=%async_computation | async-start | bytes 33554432 | tf_op jit(solution)/shard_map/all_to_all | solution.py:33
  98.0 0.0 copy-done.4
  98.0 0.1 copy.41
  98.1 0.1 reshape.79
  98.2 1.5 fusion
  99.7 0.7 all_to_all.16
  100.4 244.0 %all-to-all-done = bf16[32,64,4096]{2,1,0:T(8,128)(2,1)} async-done(((bf16[32,64,4096]{2,1,0:T(8,128)(2,1)}), bf16[32,64,4096]{2,1,0:T(8,128)(2,1)}, u32[]{:S(2)}, u32[]{:S(2)}) %all-to-all-start) | async-done | bytes 16777248 | tf_op jit(solution)/shard_map/all_to_all | solution.py:33
  344.4 48.2 %all-to-all-start.1 = ((bf16[32,1,64]{2,1,0:T(2,128)(2,1)}), bf16[32,1,64]{2,1,0:T(2,128)(2,1)S(1)}, u32[]{:S(2)}, u32[]{:S(2)}) async-start(bf16[32,1,64]{2,1,0:T(2,128)(2,1)} %all_to_all.16), calls=%async_computation.1 | async-start | bytes 32768 | tf_op jit(solution)/shard_map/all_to_all | solution.py:34
  392.5 0.0 copy-done
  392.5 0.0 copy-start.5
  392.5 12.1 %fusion.3 = f32[2048,384]{1,0:T(8,128)S(1)} fusion(bf16[2048,4096]{1,0:T(8,128)(2,1)} %bitcast.3, bf16[1,4096,384]{2,1,0:T(8,128)(2,1)S(1)} %copy-done), kind=kOutput, calls=%fused_computation.8 | convolution fusion | flops 6442450944 | bytes 23068672 | tf_op jit(solution)/shard_map/dot_general | solution.py:40
  404.6 0.0 copy-done.5
  404.6 12.6 %fusion.6 = bf16[2048,384]{1,0:T(8,128)(2,1)S(1)} fusion(bf16[2048,4096]{1,0:T(8,128)(2,1)} %bitcast.3, bf16[1,4096,384]{2,1,0:T(8,128)(2,1)S(1)} %copy-done.5, f32[2048,384]{1,0:T(8,128)S(1)} %fusion.3), kind=kOutput, calls=%fused_computation.13 | convolution fusion | flops 6447169536 | bytes 24641536 | tf_op jit(solution)/shard_map/dot_general | solution.py:41
  417.2 0.0 copy-start.2
  417.2 0.8 copy.43
  418.0 0.0 all-to-all-done.1
  418.0 3.5 stack.2
  421.4 0.0 copy-done.2
  421.4 7.1 %all-to-all-start.2 = ((bf16[4,2048,384]{1,2,0:T(8,128)(2,1)}), bf16[4,2048,384]{1,2,0:T(8,128)(2,1)}, u32[]{:S(2)}, u32[]{:S(2)}) async-start(bf16[4,2048,384]{1,2,0:T(8,128)(2,1)} %stack.2), calls=%async_computation.2 | async-start | bytes 12582912 | tf_op jit(solution)/shard_map/all_to_all | solution.py:48
  428.5 0.7 convert_reduce_fusion.1
  429.2 0.1 reshape.78
  429.3 69.1 %all-to-all-done.2 = bf16[4,2048,384]{1,2,0:T(8,128)(2,1)} async-done(((bf16[4,2048,384]{1,2,0:T(8,128)(2,1)}), bf16[4,2048,384]{1,2,0:T(8,128)(2,1)}, u32[]{:S(2)}, u32[]{:S(2)}) %all-to-all-start.2) | async-done | bytes 6291488 | tf_op jit(solution)/shard_map/all_to_all | solution.py:48
  498.4 0.0 copy-start.1
  498.4 8.6 %fusion.5 = f32[1,384,1536]{2,1,0:T(8,128)} fusion(bf16[2048,1536]{0,1:T(8,128)(2,1)} %bitcast.8, bf16[2048,384]{1,0:T(8,128)(2,1)} %copy-done.2, f32[2048]{0:T(1024)S(1)} %reshape.78, f32[]{:T(128)} %get-tuple-element.5), kind=kOutput, calls=%fused_computation.12 | convolution fusion | flops 2418868224 | bytes 10231812 | tf_op jit(solution)/shard_map/dot_general | solution.py:45
  507.0 0.0 copy-done.1
  (9 shorter events, 0.2 us)
Async XLA Ops:
  6.5 386.0 %copy-start = (bf16[1,4096,384]{2,1,0:T(8,128)(2,1)S(1)}, bf16[1,4096,384]{2,1,0:T(8,128)(2,1)}, u32[]{:S(2)}) copy-start(bf16[1,4096,384]{2,1,0:T(8,128)(2,1)} %param.12) | copy-start | bytes 9437188
  6.5 6.2 %copy-start.3 = (s32[128,8]{0,1:T(8,128)S(1)}, s32[128,8]{0,1:T(8,128)}, u32[]{:S(2)}) copy-start(s32[128,8]{0,1:T(8,128)} %param.10) | copy-start | bytes 12292
  6.5 67.3 %all-reduce.2.cloned.1.call-start = ((), (), s32[]{:S(2)}) async-start(), calls=%async_computation.3 | async-start | bytes 4194304 | tf_op jit(solution)/shard_map/psum | solution.py:10
  88.4 9.6 %copy-start.4 = (bf16[128,8]{0,1:T(8,128)(2,1)S(1)}, bf16[128,8]{0,1:T(8,128)(2,1)}, u32[]{:S(2)}) copy-start(bf16[128,8]{0,1:T(8,128)(2,1)} %param.11) | copy-start | bytes 6148
  88.4 255.9 %all-to-all-start = ((bf16[32,64,4096]{2,1,0:T(8,128)(2,1)}), bf16[32,64,4096]{2,1,0:T(8,128)(2,1)}, u32[]{:S(2)}, u32[]{:S(2)}) async-start(bf16[32,64,4096]{2,1,0:T(8,128)(2,1)} %bitcast.41), calls=%async_computation | async-start | bytes 33554432 | tf_op jit(solution)/shard_map/all_to_all | solution.py:33
  344.4 73.6 %all-to-all-start.1 = ((bf16[32,1,64]{2,1,0:T(2,128)(2,1)}), bf16[32,1,64]{2,1,0:T(2,128)(2,1)S(1)}, u32[]{:S(2)}, u32[]{:S(2)}) async-start(bf16[32,1,64]{2,1,0:T(2,128)(2,1)} %all_to_all.16), calls=%async_computation.1 | async-start | bytes 32768 | tf_op jit(solution)/shard_map/all_to_all | solution.py:34
  392.5 12.1 %copy-start.5 = (bf16[1,4096,384]{2,1,0:T(8,128)(2,1)S(1)}, bf16[1,4096,384]{2,1,0:T(8,128)(2,1)}, u32[]{:S(2)}) copy-start(bf16[1,4096,384]{2,1,0:T(8,128)(2,1)} %param.13) | copy-start | bytes 9437188
  417.2 4.3 copy-start.2
  421.4 77.0 %all-to-all-start.2 = ((bf16[4,2048,384]{1,2,0:T(8,128)(2,1)}), bf16[4,2048,384]{1,2,0:T(8,128)(2,1)}, u32[]{:S(2)}, u32[]{:S(2)}) async-start(bf16[4,2048,384]{1,2,0:T(8,128)(2,1)} %stack.2), calls=%async_computation.2 | async-start | bytes 12582912 | tf_op jit(solution)/shard_map/all_to_all | solution.py:48
  498.4 8.6 %copy-start.1 = (bf16[1,4096,384]{2,1,0:T(8,128)(2,1)S(1)}, bf16[1,4096,384]{2,1,0:T(8,128)(2,1)}, u32[]{:S(2)}) copy-start(bf16[1,4096,384]{2,1,0:T(8,128)(2,1)} %param.12) | copy-start | bytes 9437188
Sparse Core Ops, SparseCore 0:
  12.9 60.9 all-reduce.1
